TPU v7x, 32 devices: a whole 2x2x4 slice. The times are simulated.
32 devices in a mesh: fil: 8 (over z, x), row: 4 (over y, core).
Axes of the slice: x: 2, y: 2, z: 4, core: 2. Of those that a mesh axis runs over, the one named last changes fastest.
Arguments:
- images: bfloat16 [64, 2, 256, 128], P('fil', None, 'row'), may hold values from -6 to 6
- defocus: float32 [64], P('fil'), may hold values from 0.5 to 2
- references: bfloat16 [8, 2, 256, 128], P('fil', None, 'row'), may hold values from -0.0234375 to 0.0234375
- offsets: int32 [64, 32, 2], P('fil'), may hold values from -8 to 8
- posterior: int32 [64, 32], P('fil'), may hold values from 0 to 255
- class_ids: int32 [64], P('fil'), may hold values from 0 to 15
- seg_count: int32 [8], P('fil'), may hold values from 1 to 8, as said below
Outputs:
- scores: float32 [64, 32, 8], P('fil', 'row')
- averages: float32 [16, 65536], P(None, ('row', 'fil'))
Inputs may be any that keep to these rules, and one draw needn't show every extreme that they name: `seg_count`: each filament has its segments in the first slots of its 8; some filament has exactly 8.
All inputs are finite; a program needn't handle non-finite values.
Results may differ from a plain program's by a relative error of at most 0.0029.
Values may be sent and summed in bfloat16 or wider, within the bound.
A program may use at most 128 MiB of HBM per device.

v0:
```python
import math

import jax
import jax.numpy as jnp
from jax import lax
from jax.sharding import PartitionSpec as P

FROWS = 256
SHIFTS = 32
CLASSES = 16
SEG_FIL = 8


def wave_tables(shift_rows, shift_cols, row_freq, col_freq, box):
    row_angle = (shift_rows[..., None] * row_freq % box).astype(jnp.float32) * (
        -2.0 * math.pi / box
    )
    col_angle = (shift_cols[..., None] * col_freq % box).astype(jnp.float32) * (
        -2.0 * math.pi / box
    )
    row_cos = jnp.cos(row_angle)[..., :, None]
    row_sin = jnp.sin(row_angle)[..., :, None]
    col_cos = jnp.cos(col_angle)[..., None, :]
    col_sin = jnp.sin(col_angle)[..., None, :]
    phase_re = row_cos * col_cos - row_sin * col_sin
    phase_im = row_cos * col_sin + row_sin * col_cos
    return (phase_re, phase_im)


def contrast(defocus_vals, row_freq, col_freq, box):
    radius = (row_freq[:, None] * row_freq[:, None] + col_freq[None, :] * col_freq[None, :]).astype(
        jnp.float32
    ) / float(box * box)
    return -jnp.sin(200.0 * defocus_vals[:, None, None] * radius[None] + 0.1)


def aligned_rows(block_images, gain, block_offsets, row_freq, col_freq, box):
    phase_re, phase_im = wave_tables(
        block_offsets[..., 0], block_offsets[..., 1], row_freq, col_freq, box
    )
    scaled = gain[:, None]
    real_part = block_images[:, 0].astype(jnp.float32)[:, None]
    imag_part = block_images[:, 1].astype(jnp.float32)[:, None]
    aligned_re = scaled * (real_part * phase_re - imag_part * phase_im)
    aligned_im = scaled * (real_part * phase_im + imag_part * phase_re)
    stacked = jnp.stack([aligned_re, aligned_im], axis=3).astype(jnp.bfloat16)
    return stacked.reshape(stacked.shape[0] * stacked.shape[1], -1)


def correlate(aligned, panel):
    return lax.dot_general(
        aligned, panel, (((1,), (1,)), ((), ())), preferred_element_type=jnp.float32
    )


def per_device(images, defocus, references, offsets, posterior, class_ids, seg_count):
    seg_dev = images.shape[0]
    rows = images.shape[2]
    cols = images.shape[3]
    box = FROWS
    row_first = lax.axis_index("row") * rows
    row_freq = (row_first + jnp.arange(rows, dtype=jnp.int32) + box // 2) % box - box // 2
    col_freq = jnp.arange(cols, dtype=jnp.int32)
    live = (
        (jnp.arange(SEG_FIL, dtype=jnp.int32)[None, :] < seg_count[:, None])
        .reshape(-1)
        .astype(jnp.float32)
    )
    weight = live[:, None] * posterior.astype(jnp.float32) / 256.0
    local_panel = jnp.transpose(references, (0, 2, 1, 3)).reshape(references.shape[0], -1)
    classes = jnp.arange(CLASSES, dtype=jnp.int32)
    blocks = seg_dev // 8
    panel = lax.all_gather(local_panel, "fil", axis=0, tiled=True)

    def step(carry, inputs):
        numer, denom = carry
        block_images, block_defocus, block_offsets, block_weight, block_live, block_ids = inputs
        ctf = contrast(block_defocus, row_freq, col_freq, box)
        aligned = aligned_rows(
            block_images, ctf * block_live[:, None, None], block_offsets, row_freq, col_freq, box
        )
        block_scores = correlate(aligned, panel)
        member = (block_ids[None, :] == classes[:, None]).astype(jnp.float32)
        spread = (member[:, :, None] * block_weight[None]).astype(jnp.bfloat16).reshape(CLASSES, -1)
        numer = numer + jnp.dot(spread, aligned, preferred_element_type=jnp.float32)
        totals = member * jnp.sum(block_weight, axis=1)[None, :]
        denom = denom + jnp.dot(
            totals,
            (ctf * ctf).reshape(ctf.shape[0], -1),
            precision=lax.Precision.HIGHEST,
            preferred_element_type=jnp.float32,
        )
        return ((numer, denom), block_scores.reshape(8, SHIFTS, -1))

    inputs = (
        images.reshape(blocks, 8, 2, rows, cols),
        defocus.reshape(blocks, 8),
        offsets.reshape(blocks, 8, SHIFTS, 2),
        weight.reshape(blocks, 8, SHIFTS),
        live.reshape(blocks, 8),
        class_ids.reshape(blocks, 8),
    )
    start = (
        jnp.zeros((CLASSES, rows * 2 * cols), jnp.float32),
        jnp.zeros((CLASSES, rows * cols), jnp.float32),
    )
    (numer, denom), partial_scores = lax.scan(step, start, inputs)
    scores = lax.psum_scatter(
        partial_scores.reshape(seg_dev, SHIFTS, -1), "row", scatter_dimension=1, tiled=True
    )
    share = rows * 2 * cols // lax.axis_size("fil")
    total_numer, total_denom = lax.psum((numer, denom), "fil")
    wide = jnp.broadcast_to(
        total_denom.reshape(CLASSES, rows, 1, cols), (CLASSES, rows, 2, cols)
    ).reshape(CLASSES, -1)
    whole_avg = total_numer * lax.rsqrt(wide + 1.0)
    averages = lax.dynamic_slice_in_dim(whole_avg, lax.axis_index("fil") * share, share, 1)
    return (scores, averages)


def solution(mesh):
    placed = (
        P("fil", None, "row", None),
        P("fil"),
        P("fil", None, "row", None),
        P("fil", None, None),
        P("fil", None),
        P("fil"),
        P("fil"),
    )
    return jax.shard_map(
        per_device,
        mesh=mesh,
        in_specs=placed,
        out_specs=(P("fil", "row", None), P(None, ("row", "fil"))),
        check_vma=False,
    )
```

profile of v0, /device:TPU:0, one launch (start us, length us, event | category | flops | bytes accessed | tf_op | source)
XLA Modules:
  0.0 172.7 jit_solution(13478070120144497746)
XLA Ops:
  8.1 1.0 bitcast_convert_fusion.1
  9.1 0.8 fusion.37
  9.9 0.6 fusion.21
  11.1 0.7 broadcast_multiply_fusion
  11.8 0.6 fusion.23
  12.5 0.9 negate_multiply_fusion
  13.4 6.8 %subtract_multiply_fusion = (bf16[8,32,64,1,128]{4,2,3,1,0:T(8,128)(2,1)S(1)}, bf16[8,32,64,1,128]{4,2,3,1,0:T(8,128)(2,1)}) fusion(f32[8,64,128]{2,1,0:T(8,128)S(1)} %get-tuple-element.37, f32[8,32,128]{2,1,0:T(8,128)S(1)} %get-tuple-element.57, f32[8,32,64]{2,1,0:T(8,128)S(1)} %get-tuple-element.41, f32[8,32,128]{2,1,0:T(8,128)S(1)} %get-tuple-element.56, ...), kind=kLoop, calls=%fused_computation.2 | loop fusion | flops 33554432 | bytes 9568256 | tf_op jit(solution)/shard_map/while/body/eval_jaxpr/mul | solution.py:44
  20.2 6.4 %maximum_convert_fusion = bf16[8,32,64,2,128]{4,2,3,1,0:T(8,128)(2,1)} fusion(bf16[8,32,64,1,128]{4,2,3,1,0:T(8,128)(2,1)} %get-tuple-element.35, bf16[8,32,64,1,128]{4,2,3,1,0:T(8,128)(2,1)S(1)} %get-tuple-element.34), kind=kLoop, calls=%fused_computation | loop fusion | flops 4194304 | bytes 16777216 | tf_op jit(solution)/shard_map/while/body/eval_jaxpr/convert_element_type | solution.py:46
  26.6 16.4 %copy.13 = bf16[8,32,64,2,128]{4,3,2,1,0:T(2,128)(2,1)} copy(bf16[8,32,64,2,128]{4,2,3,1,0:T(8,128)(2,1)} %maximum_convert_fusion) | data formatting | bytes 16777216 | tf_op jit(solution)/shard_map/while/body/eval_jaxpr/convert_element_type | solution.py:46
  43.0 0.1 add.184
  43.1 0.2 fusion.36
  43.4 0.1 convert_element_type.98
  43.5 14.5 %convert_element_type.99 = bf16[256,16384]{1,0:T(8,128)(2,1)} reshape(bf16[8,32,64,2,128]{4,3,2,1,0:T(2,128)(2,1)} %copy.13) | data formatting | bytes 16777216 | tf_op jit(solution)/shard_map/while/body/eval_jaxpr/convert_element_type | solution.py:46
  58.0 2.2 %fusion.3 = f32[16,8192]{1,0:T(8,128)} fusion(f32[8192]{0:T(1024)S(1)} %fusion.25, f32[8]{0:T(128)S(1)} %broadcast_multiply_fusion, f32[8]{0:T(128)S(1)} %get-tuple-element.32, s32[8]{0:T(128)S(1)} %copy-done.2), kind=kOutput, calls=%fused_computation.9 | convolution fusion | flops 12779776 | bytes 557152 | tf_op jit(solution)/shard_map/while/body/eval_jaxpr/dot_general | solution.py:87
  60.3 5.6 %fusion.38 = f32[16,16384]{1,0:T(8,128)} fusion(bf16[16,256]{1,0:T(8,128)(2,1)S(1)} %convert_element_type.98, bf16[256,16384]{1,0:T(8,128)(2,1)} %convert_element_type.99), kind=kOutput, calls=%fused_computation.67 | convolution fusion | flops 134217728 | bytes 9445376 | tf_op jit(solution)/shard_map/while/body/eval_jaxpr/dot_general | solution.py:85
  65.9 14.6 %convert_element_type.94 = bf16[8,32,16384]{2,1,0:T(8,128)(2,1)} reshape(bf16[8,32,64,2,128]{4,3,2,1,0:T(2,128)(2,1)} %copy.13) | data formatting | bytes 16777216 | tf_op jit(solution)/shard_map/while/body/eval_jaxpr/convert_element_type | solution.py:46
  80.6 34.3 %all-gather = bf16[8,1,16384]{2,1,0:T(2,128)(2,1)S(1)} all-gather(bf16[1,1,16384]{2,1,0:T(2,128)(2,1)S(1)} %reshape.286), channel_id=1, replica_groups=mesh['fil'=8,'row'=4] {'fil'}, dimensions={0}, use_global_device_ids=true | all-gather | bytes 294912 | tf_op jit(solution)/shard_map/all_gather | solution.py:73
  114.9 6.4 %fusion = f32[8,32,8]{2,1,0:T(8,128)} fusion(bf16[8,32,16384]{2,1,0:T(8,128)(2,1)} %convert_element_type.94, bf16[8,1,16384]{2,1,0:T(2,128)(2,1)S(1)} %all-gather), kind=kOutput, calls=%fused_computation.6 | convolution fusion | flops 67108864 | bytes 8658944 | tf_op jit(solution)/shard_map/while/body/eval_jaxpr/dot_general | solution.py:51
  121.3 40.0 %all-reduce.3.cloned.1.call-done = (f32[16,8192]{1,0:T(8,128)}, f32[16,16384]{1,0:T(8,128)}) async-done(((f32[16,8192]{1,0:T(8,128)}, f32[16,16384]{1,0:T(8,128)}), (f32[16,8192]{1,0:T(8,128)}, f32[16,16384]{1,0:T(8,128)})) %all-reduce.3.cloned.1.call-update) | async-done | bytes 1572880 | tf_op jit(solution)/shard_map/psum | solution.py:112
  161.3 1.1 rsqrt_bitcast_fusion
  162.4 0.1 copy.17
  162.5 0.4 broadcast_in_dim.21
  162.9 0.8 rsqrt.12
  163.7 1.6 dynamic-slice_multiply_fusion
  (20 shorter events, 0.4 us)
Async XLA Ops:
  8.0 153.3 %all-reduce.3.cloned.1.call-start = ((), (), s32[]{:S(2)}) async-start(), calls=%async_computation.2 | async-start | bytes 3145728 | tf_op jit(solution)/shard_map/psum | solution.py:112
  26.6 16.5 %copy-start.1 = (s32[8,32]{1,0:T(8,128)S(1)}, s32[8,32]{1,0:T(8,128)}, u32[]{:S(2)}) copy-start(s32[8,32]{1,0:T(8,128)} %param.11) | copy-start | bytes 3076
  26.6 16.7 %copy-start.2 = (s32[8]{0:T(128)S(1)}, s32[8]{0:T(128)}, u32[]{:S(2)}) copy-start(s32[8]{0:T(128)} %param.12) | copy-start | bytes 100
  65.9 14.7 %copy-start = (bf16[1,2,64,128]{3,2,1,0:T(8,128)(2,1)S(1)}, bf16[1,2,64,128]{3,2,1,0:T(8,128)(2,1)}, u32[]{:S(2)}) copy-start(bf16[1,2,64,128]{3,2,1,0:T(8,128)(2,1)} %param.9) | copy-start | bytes 98308
  65.9 99.4 %reduce-scatter.2.cloned.1.call-start = ((), (), s32[]{:S(2)}) async-start(), calls=%async_computation.1 | async-start | bytes 163840 | tf_op jit(solution)/shard_map/reduce_scatter | solution.py:108
Sparse Core Ops, SparseCore 0:
  66.0 95.2 all-reduce.2
Sparse Core Ops, SparseCore 1:
  121.4 20.7 reduce-scatter.1
where the time goes:
time: 174 us; the launch traced here: 173 us
  local copies, waits for them, and re-layouts  47.9 us (28%)
  waiting for transfers between devices  40 us (23%)
  blocking collectives  34.3 us (20%)
  other arithmetic  20 us (11%)
  between operations  16.3 us (9%)
  matrix products  14.2 us (8%)
    convert_element_type x3, local copies, waits for them, and re-layouts, aligned_rows(): stacked = jnp.stack([aligned_re, aligned_im], axis=3).astype(jnp.bfloat16)  45.5 us
    psum x1, waiting for transfers between devices, per_device(): total_numer, total_denom = lax.psum((numer, denom), 'fil')  40 us
    all_gather x1, blocking collectives, per_device(): panel = lax.all_gather(local_panel, 'fil', axis=0, tiled=True)  34.3 us
    mul x2, other arithmetic, aligned_rows(): aligned_re = scaled * (real_part * phase_re - imag_part * phase_im)  7.83 us
    dot_general x1, matrix products, correlate(): lax.dot_general(aligned, panel, (((1,), (1,)), ((), ())), preferred_eleme...  6.38 us
    convert_element_type x1, other arithmetic, aligned_rows(): stacked = jnp.stack([aligned_re, aligned_im], axis=3).astype(jnp.bfloat16)  6.36 us
    dot_general x1, matrix products, step(): numer = numer + jnp.dot(spread, aligned, preferred_element_type=jnp.float32)  5.56 us
  transfers between devices with their start and end apart: 2, of which 1 were waited for; matrix products, arithmetic and copies ran while one was open for 15% of the time, Pallas kernels for 0%

commit v1 on v0

--- a/solution.py
+++ b/solution.py
@@ -3,7 +3,11 @@
 import jax
 import jax.numpy as jnp
 from jax import lax
+from jax.experimental import pallas as pl
+from jax.experimental.pallas import tpu as pltpu
 from jax.sharding import PartitionSpec as P
+
+MESH = pl.DeviceIdType.MESH
 
 FROWS = 256
 SHIFTS = 32
@@ -118,6 +122,327 @@
     return (scores, averages)
 
 
+SINE = (
+    6.283185139080197,
+    -41.34161488788259,
+    81.60061435566797,
+    -76.62117706362086,
+    41.37130756865165,
+    -12.514333309608835,
+)
+DEFOCUS, TOTAL, LIVE = 16, 17, 18
+
+
+def sine_turns(turns):
+    r = turns - jnp.round(turns)
+    z = r * r
+    p = jnp.full_like(z, SINE[-1])
+    for c in SINE[-2::-1]:
+        p = p * z + c
+    return p * r
+
+
+def floats(shape, axis):
+    return lax.broadcasted_iota(jnp.int32, shape, axis).astype(jnp.float32)
+
+
+def split(x):
+    hi = x.astype(jnp.bfloat16)
+    return hi, (x - hi.astype(jnp.float32)).astype(jnp.bfloat16)
+
+
+def mm(a, b, contract_a=1):
+    return lax.dot_general(
+        a, b, (((contract_a,), (0,)), ((), ())), preferred_element_type=jnp.float32
+    )
+
+
+def ctf_of(defocus, kw, kx, box):
+    radius = (kw * kw + kx * kx) * (1.0 / (box * box))
+    arg = 200.0 * defocus * radius + 0.1
+    return -sine_turns(arg * (0.5 / math.pi))
+
+
+def fused(
+    fils,
+    row_devs,
+    img,
+    refs,
+    tile,
+    cols,
+    scores_out,
+    avg_out,
+    refs_all,
+    tiles_all,
+    pf,
+    pbuf,
+    precv,
+    fbuf,
+    yscr,
+    sbuf,
+    srecv,
+    ref_send,
+    ref_recv,
+    tile_send,
+    tile_recv,
+    p_send,
+    p_recv,
+    s_send,
+    s_recv,
+):
+    segs, _, rows, kcols = img.shape
+    box = FROWS
+    own = rows // fils
+    fil = lax.axis_index("fil")
+    row = lax.axis_index("row")
+
+    def fil_peer(k):
+        return lax.rem(fil + k, fils)
+
+    def row_peer(k):
+        return lax.rem(row + k, row_devs)
+
+    barrier = pltpu.get_barrier_semaphore()
+    for k in range(1, fils):
+        pl.semaphore_signal(barrier, inc=1, device_id=(fil_peer(k), row), device_id_type=MESH)
+    for k in range(1, row_devs):
+        pl.semaphore_signal(barrier, inc=1, device_id=(fil, row_peer(k)), device_id_type=MESH)
+    pl.semaphore_wait(barrier, fils + row_devs - 2)
+
+    def to_fil(k, src, dst_all, send, recv):
+        return pltpu.make_async_remote_copy(
+            src_ref=src,
+            dst_ref=dst_all.at[fil],
+            send_sem=send.at[k],
+            recv_sem=recv.at[fil],
+            device_id=(fil_peer(k), row),
+            device_id_type=MESH,
+        )
+
+    def from_fil(k, dst_all, send, recv):
+        d = fil_peer(k)
+        return pltpu.make_async_remote_copy(
+            src_ref=dst_all.at[d],
+            dst_ref=dst_all.at[d],
+            send_sem=send.at[k],
+            recv_sem=recv.at[d],
+            device_id=(d, row),
+            device_id_type=MESH,
+        )
+
+    tile_copies = [to_fil(k, tile, tiles_all, tile_send, tile_recv) for k in range(1, fils)]
+    ref_copies = [to_fil(k, refs, refs_all, ref_send, ref_recv) for k in range(1, fils)]
+    for c in tile_copies + ref_copies:
+        c.start()
+    tiles_all[fil] = tile[...]
+    refs_all[fil] = refs[...]
+
+    pairs = segs * SHIFTS
+    sy = cols[:, 0:1]
+    sx = cols[:, 1:2]
+    wt = cols[:, 2:3]
+    lane = lax.broadcasted_iota(jnp.int32, (1, 2 * rows), 1)
+    ky = (row * rows + lax.rem(lane, rows)).astype(jnp.float32)
+    kw = jnp.where(ky >= box // 2, ky - box, ky)
+    low = lane < rows
+    q = -(sy * kw)
+    wave_a = sine_turns((q + jnp.where(low, 64.0, 128.0)) * (1.0 / box))
+    wave_b = sine_turns((q + jnp.where(low, 0.0, 64.0)) * (1.0 / box))
+    kx = floats((1, kcols), 1)
+    qc = -(sx * kx)
+    col_cos = sine_turns((qc + 64.0) * (1.0 / box))
+    col_sin = sine_turns(qc * (1.0 / box))
+
+    a_hi, a_lo = split(wave_a)
+    b_hi, b_lo = split(wave_b)
+    c_hi, c_lo = split(jnp.concatenate([col_cos * wt, col_sin * wt], axis=1))
+
+    kyl = (row * rows).astype(jnp.float32) + floats((rows, 1), 0)
+    kwl = jnp.where(kyl >= box // 2, kyl - box, kyl)
+    gains = []
+    for i in range(segs):
+        ctf = ctf_of(tile[i : i + 1, DEFOCUS : DEFOCUS + 1], kwl, kx, box)
+        g = ctf * tile[i : i + 1, LIVE : LIVE + 1]
+        g_re = g * img[i, 0].astype(jnp.float32)
+        g_im = g * img[i, 1].astype(jnp.float32)
+        gains.append((g_re, g_im))
+        at = slice(i * SHIFTS, (i + 1) * SHIFTS)
+        grid = mm(
+            jnp.concatenate([a_hi[at], a_hi[at], a_lo[at]], axis=0),
+            jnp.concatenate([c_hi[at], c_lo[at], c_hi[at]], axis=0),
+            contract_a=0,
+        )
+        w_re = grid[:rows, :kcols] + grid[rows:, kcols:]
+        w_im = grid[:rows, kcols:] - grid[rows:, :kcols]
+        p_re = g_re * w_re - g_im * w_im
+        p_im = g_re * w_im + g_im * w_re
+        for d in range(fils):
+            part = slice(d * own, (d + 1) * own)
+            pf[d, pl.ds(i, own, stride=2 * segs), :] = p_re[part]
+            pf[d, pl.ds(segs + i, own, stride=2 * segs), :] = p_im[part]
+
+    p_copies = []
+    for k in range(1, fils):
+        d = fil_peer(k)
+        pbuf[d] = pf[d].astype(jnp.bfloat16)
+        c = to_fil(k, pbuf.at[d], precv, p_send, p_recv)
+        c.start()
+        p_copies.append(c)
+    precv[fil] = pf[fil].astype(jnp.bfloat16)
+
+    for k in range(1, fils):
+        from_fil(k, refs_all, ref_send, ref_recv).wait_recv()
+    for i in range(segs):
+        at = slice(i * SHIFTS, (i + 1) * SHIFTS)
+        lhs = jnp.concatenate([a_hi[at], b_hi[at], a_lo[at], b_lo[at]], axis=0)
+        g_re, g_im = gains[i]
+        for r in range(0, fils, 2):
+            panel = []
+            for e in (r, r + 1):
+                f_re = refs_all[e, 0].astype(jnp.float32)
+                f_im = refs_all[e, 1].astype(jnp.float32)
+                q_re = g_re * f_re + g_im * f_im
+                q_im = g_im * f_re - g_re * f_im
+                panel.append(jnp.concatenate([q_re, q_im], axis=0).astype(jnp.bfloat16))
+            z = mm(lhs, jnp.concatenate(panel, axis=1))
+            z = z[: 2 * SHIFTS] + z[2 * SHIFTS :]
+            for e in (0, 1):
+                ze = z[:, e * kcols : (e + 1) * kcols]
+                fbuf[at, (r + e) * kcols : (r + e + 1) * kcols] = (
+                    col_cos[at] * ze[:SHIFTS] - col_sin[at] * ze[SHIFTS:]
+                )
+    f_hi, f_lo = split(fbuf[...])
+    wide = (fils * kcols, 128)
+    ones = (
+        lax.broadcasted_iota(jnp.int32, wide, 0) // kcols
+        == lax.rem(lax.broadcasted_iota(jnp.int32, wide, 1), fils)
+    ).astype(jnp.bfloat16)
+    spread = mm(f_hi, ones) + mm(f_lo, ones)
+    per = SHIFTS // row_devs
+    pick = (
+        lax.broadcasted_iota(jnp.int32, (per, 128), 1) // fils
+        == lax.broadcasted_iota(jnp.int32, (per, 128), 0)
+    ).astype(jnp.float32)
+    yscr[...] = jnp.sum(spread.reshape(pairs // per, per, 128) * pick[None], axis=1)
+    for j in range(row_devs):
+        sbuf[j] = yscr[pl.ds(j, segs, stride=row_devs), :]
+    s_copies = []
+    for k in range(1, row_devs):
+        c = pltpu.make_async_remote_copy(
+            src_ref=sbuf.at[row_peer(k)],
+            dst_ref=srecv.at[row],
+            send_sem=s_send.at[k],
+            recv_sem=s_recv.at[row],
+            device_id=(fil, row_peer(k)),
+            device_id_type=MESH,
+        )
+        c.start()
+        s_copies.append(c)
+
+    for k in range(1, fils):
+        from_fil(k, tiles_all, tile_send, tile_recv).wait_recv()
+    every = fils * segs
+    tiles = tiles_all[...].reshape(every, 128)
+    member = jnp.transpose(tiles)[:CLASSES].astype(jnp.bfloat16)
+    defocus = tiles[:, DEFOCUS : DEFOCUS + 1]
+    total = tiles[:, TOTAL : TOTAL + 1]
+    squares = []
+    for y in range(own):
+        k0 = (row * rows + fil * own + y).astype(jnp.float32)
+        k0 = jnp.where(k0 >= box // 2, k0 - box, k0)
+        ctf = ctf_of(defocus, k0, kx, box)
+        squares.append(total * (ctf * ctf))
+    d_hi, d_lo = split(jnp.concatenate(squares, axis=1))
+    denom = mm(member, d_hi) + mm(member, d_lo)
+    scale = lax.rsqrt(denom + 1.0)
+
+    for k in range(1, fils):
+        from_fil(k, precv, p_send, p_recv).wait_recv()
+    parts = precv[...].astype(jnp.float32).reshape(fils, 2 * own, segs, kcols)
+    for y in range(own):
+        for part in range(2):
+            t = 2 * y + part
+            rhs = parts[:, t].reshape(every, kcols).astype(jnp.bfloat16)
+            avg_out[:, t * kcols : (t + 1) * kcols] = (
+                mm(member, rhs) * scale[:, y * kcols : (y + 1) * kcols]
+            )
+
+    acc = sbuf[row]
+    for k in range(1, row_devs):
+        q = row_peer(k)
+        pltpu.make_async_remote_copy(
+            src_ref=srecv.at[q],
+            dst_ref=srecv.at[q],
+            send_sem=s_send.at[k],
+            recv_sem=s_recv.at[q],
+            device_id=(fil, q),
+            device_id_type=MESH,
+        ).wait_recv()
+        acc = acc + srecv[q]
+    scores_out[...] = acc
+    for c in tile_copies + ref_copies + p_copies + s_copies:
+        c.wait_send()
+
+
+def per_device_fused(images, defocus, references, offsets, posterior, class_ids, seg_count):
+    segs, _, rows, kcols = images.shape
+    fils = lax.axis_size("fil")
+    row_devs = lax.axis_size("row")
+    live = (jnp.arange(SEG_FIL, dtype=jnp.int32) < seg_count).astype(jnp.float32)
+    weight = posterior.astype(jnp.float32) / 256.0
+    member = (class_ids[:, None] == jnp.arange(CLASSES, dtype=jnp.int32)[None]).astype(jnp.float32)
+    numbers = jnp.stack([defocus, live * jnp.sum(weight, axis=1), live], axis=1)
+    tile = jnp.pad(jnp.concatenate([member, numbers], axis=1), ((0, 0), (0, 125 - CLASSES)))
+    shifts = offsets.astype(jnp.float32).reshape(segs * SHIFTS, 2)
+    cols = jnp.concatenate([shifts, weight.reshape(segs * SHIFTS, 1)], axis=1)
+    own = rows // fils
+    block = 2 * own * segs
+    per = SHIFTS // row_devs
+    vmem = pl.BlockSpec(memory_space=pltpu.VMEM)
+    dma = pltpu.SemaphoreType.DMA
+
+    def kernel(*refs):
+        fused(fils, row_devs, *refs)
+
+    scores, averages = pl.pallas_call(
+        kernel,
+        out_shape=(
+            jax.ShapeDtypeStruct((segs, 128), jnp.float32),
+            jax.ShapeDtypeStruct((CLASSES, 2 * own * kcols), jnp.float32),
+        ),
+        in_specs=[vmem] * 4,
+        out_specs=(vmem, vmem),
+        scratch_shapes=[
+            pltpu.VMEM((fils, 2, rows, kcols), jnp.bfloat16),
+            pltpu.VMEM((fils, segs, 128), jnp.float32),
+            pltpu.VMEM((fils, block, kcols), jnp.float32),
+            pltpu.VMEM((fils, block, kcols), jnp.bfloat16),
+            pltpu.VMEM((fils, block, kcols), jnp.bfloat16),
+            pltpu.VMEM((segs * SHIFTS, fils * kcols), jnp.float32),
+            pltpu.VMEM((segs * row_devs, 128), jnp.float32),
+            pltpu.VMEM((row_devs, segs, 128), jnp.float32),
+            pltpu.VMEM((row_devs, segs, 128), jnp.float32),
+            dma((fils,)),
+            dma((fils,)),
+            dma((fils,)),
+            dma((fils,)),
+            dma((fils,)),
+            dma((fils,)),
+            dma((row_devs,)),
+            dma((row_devs,)),
+        ],
+        compiler_params=pltpu.CompilerParams(
+            collective_id=0, has_side_effects=True, vmem_limit_bytes=32 * 1024 * 1024
+        ),
+    )(images, references[0], tile, cols)
+    return scores[:, : per * fils].reshape(segs, per, fils), averages
+
+
+def fits(mesh):
+    fils, row_devs = mesh.shape["fil"], mesh.shape["row"]
+    return fils == 8 and FROWS == 8 * fils * row_devs and SHIFTS == 8 * row_devs
+
+
 def solution(mesh):
     placed = (
         P("fil", None, "row", None),
@@ -129,7 +454,7 @@
         P("fil"),
     )
     return jax.shard_map(
-        per_device,
+        per_device_fused if fits(mesh) else per_device,
         mesh=mesh,
         in_specs=placed,
         out_specs=(P("fil", "row", None), P(None, ("row", "fil"))),

time: 174 us -> 27 us (0.16)
  the two profiles are of different devices: /device:TPU:0 before, /device:TPU:27 now
where the time goes in v1:
time: 27 us; the launch traced here: 26.7 us
  Pallas kernels  19.8 us (73%)
  local copies, waits for them, and re-layouts  3.22 us (12%)
  other arithmetic  2.37 us (9%)
  between operations  1.34 us (5%)
    pallas_call x1, Pallas kernels, per_device_fused(): pl.pallas_call(kernel, out_shape=(jax.ShapeDtypeStruct((segs, 128), jnp.f...  19.8 us
    unnamed x5, local copies, waits for them, and re-layouts  1.41 us
    div x1, other arithmetic, per_device_fused(): weight = posterior.astype(jnp.float32) / 256.0  0.84 us
    another operation x1, local copies, waits for them, and re-layouts, per_device_fused(): numbers = jnp.stack([defocus, live * jnp.sum(weight, axis=1), live], axis=1)  0.73 us
    convert_element_type x1, other arithmetic, per_device_fused(): (class_ids[:, None] == jnp.arange(CLASSES, dtype=jnp.int32)[None]).astype...  0.72 us
    convert_element_type x1, other arithmetic, per_device_fused(): shifts = offsets.astype(jnp.float32).reshape(segs * SHIFTS, 2)  0.7 us
    reshape x1, local copies, waits for them, and re-layouts, per_device_fused(): return (scores[:, :per * fils].reshape(segs, per, fils), averages)  0.69 us

profile of v1, /device:TPU:27, one launch (start us, length us, event | category | flops | bytes accessed | tf_op | source)
XLA Modules:
  0.0 26.7 jit_solution(2408538524489187234)
XLA Ops:
  0.6 0.0 copy-start
  0.6 0.8 %convert_multiply_fusion = (f32[8,32]{1,0:T(8,128)S(1)}, f32[8]{0:T(128)S(1)}) fusion(s32[8,32]{1,0:T(8,128)} %param.11), kind=kLoop, calls=%fused_computation.5 | loop fusion | flops 760 | bytes 2080 | tf_op jit(solution)/shard_map/div | solution.py:392
  1.5 0.1 copy.16
  2.2 0.7 %copy.17 = f32[8,1]{1,0:T(8,128)S(1)} copy(f32[8,1]{0,1:T(1,128)} %bitcast.12) | data formatting | bytes 64 | tf_op jit(solution)/shard_map/stack | solution.py:394
  3.0 0.7 %fusion.2 = f32[8,16]{1,0:T(8,128)S(1)} fusion(s32[8]{0:T(128)} %param.12), kind=kLoop, calls=%fused_computation.10 | loop fusion | flops 256 | bytes 544 | tf_op jit(solution)/shard_map/convert_element_type | solution.py:393
  3.7 0.1 select_maximum_fusion.refs_2_
  3.8 0.1 reshape.33
  3.9 0.7 %convert_element_type.24 = f32[8,32,2]{1,2,0:T(2,128)S(1)} convert(s32[8,32,2]{1,2,0:T(2,128)} %param.10) | non-fusion elementwise | flops 512 | bytes 4096 | tf_op jit(solution)/shard_map/convert_element_type | solution.py:396
  4.6 0.1 reshape.32
  4.7 0.1 copy.19.refs_3_
  4.8 0.0 copy-done
  4.8 0.0 copy-start.1
  4.8 0.7 %copy-done.1 = bf16[1,2,64,128]{3,2,1,0:T(8,128)(2,1)S(1)} copy-done((bf16[1,2,64,128]{3,2,1,0:T(8,128)(2,1)S(1)}, bf16[1,2,64,128]{3,2,1,0:T(8,128)(2,1)}, u32[]{:S(2)}) %copy-start.1) | copy-done | bytes 32792
  5.6 19.8 %shard_map.86 = (f32[8,128]{1,0:T(8,128)S(1)}, f32[16,2048]{1,0:T(8,128)S(1)}) custom-call(bf16[8,2,64,128]{3,2,1,0:T(8,128)(2,1)S(1)} %copy-done, bf16[2,64,128]{2,1,0:T(8,128)(2,1)S(1)} %bitcast.9, f32[8,128]{1,0:T(8,128)S(1)} %select_maximum_fusion.refs_2_, f32[256,3]{1,0:T(8,128)S(1)} %copy.19.refs_3_), custom_call_target="tpu_custom_call" | custom-call | tf_op jit(solution)/shard_map/pallas_call | solution.py:407
  25.4 0.7 %reshape.34 = f32[8,8,8]{2,1,0:T(8,128)} reshape(f32[8,64]{1,0:T(8,128)S(1)} %bitcast.10) | data formatting | bytes 4096 | tf_op jit(solution)/shard_map/reshape | solution.py:438
  26.1 0.7 %copy.22 = f32[16,2048]{1,0:T(8,128)} copy(f32[16,2048]{1,0:T(8,128)S(1)} %get-tuple-element.11) | data formatting | bytes 262144
  (4 shorter events, 0.0 us)
Async XLA Ops:
  0.6 4.2 %copy-start = (bf16[8,2,64,128]{3,2,1,0:T(8,128)(2,1)S(1)}, bf16[8,2,64,128]{3,2,1,0:T(8,128)(2,1)}, u32[]{:S(2)}) copy-start(bf16[8,2,64,128]{3,2,1,0:T(8,128)(2,1)} %refs_0_.1) | copy-start | bytes 786436
  4.8 0.8 %copy-start.1 = (bf16[1,2,64,128]{3,2,1,0:T(8,128)(2,1)S(1)}, bf16[1,2,64,128]{3,2,1,0:T(8,128)(2,1)}, u32[]{:S(2)}) copy-start(bf16[1,2,64,128]{3,2,1,0:T(8,128)(2,1)} %param.9) | copy-start | bytes 98308

commit v2 on v1

--- a/solution.py
+++ b/solution.py
@@ -166,12 +166,23 @@
 def fused(
     fils,
     row_devs,
-    img,
+    img_hbm,
     refs,
-    tile,
-    cols,
+    offsets_hbm,
+    posterior_hbm,
+    defocus_hbm,
+    ids_hbm,
+    count_hbm,
     scores_out,
     avg_out,
+    img,
+    offsets,
+    posterior,
+    defocus_in,
+    ids_in,
+    count_in,
+    turned,
+    tile,
     refs_all,
     tiles_all,
     pf,
@@ -189,6 +200,7 @@
     p_recv,
     s_send,
     s_recv,
+    in_sem,
 ):
     segs, _, rows, kcols = img.shape
     box = FROWS
@@ -207,6 +219,22 @@
         pl.semaphore_signal(barrier, inc=1, device_id=(fil_peer(k), row), device_id_type=MESH)
     for k in range(1, row_devs):
         pl.semaphore_signal(barrier, inc=1, device_id=(fil, row_peer(k)), device_id_type=MESH)
+    pulls = [
+        pltpu.make_async_copy(src, dst, in_sem.at[j])
+        for j, (src, dst) in enumerate(
+            (
+                (offsets_hbm, offsets),
+                (posterior_hbm, posterior),
+                (defocus_hbm, defocus_in),
+                (ids_hbm, ids_in),
+                (count_hbm, count_in),
+                (img_hbm, img),
+                (refs, refs_all.at[fil]),
+            )
+        )
+    ]
+    for c in pulls:
+        c.start()
     pl.semaphore_wait(barrier, fils + row_devs - 2)
 
     def to_fil(k, src, dst_all, send, recv):
@@ -230,17 +258,59 @@
             device_id_type=MESH,
         )
 
+    partner = fil + 1 - 2 * lax.rem(fil, 2)
+    ref_copies = []
+    for k in range(fils // 2, 0, -1):
+        d = fil_peer(2 * k) if 2 * k < fils else partner
+        ref_copies.append(
+            pltpu.make_async_remote_copy(
+                src_ref=refs,
+                dst_ref=refs_all.at[fil],
+                send_sem=ref_send.at[k],
+                recv_sem=ref_recv.at[fil],
+                device_id=(d, row),
+                device_id_type=MESH,
+            )
+        )
+    for c in ref_copies:
+        c.start()
+
+    for c in pulls[:5]:
+        c.wait()
+    turned[...] = jnp.zeros_like(turned)
+    shifts = offsets[...].astype(jnp.float32)
+    turned[0:segs, 0:SHIFTS] = shifts[:, 0, :]
+    turned[segs : 2 * segs, 0:SHIFTS] = shifts[:, 1, :]
+    turned[2 * segs : 3 * segs, 0:SHIFTS] = posterior[...].astype(jnp.float32) * (1.0 / 256.0)
+    turned[3 * segs : 3 * segs + 1, 0:segs] = ids_in[...].astype(jnp.float32)
+    turned[3 * segs + 1 : 3 * segs + 2, 0:segs] = defocus_in[...]
+    up = jnp.transpose(turned[...])
+    weights = turned[2 * segs : 3 * segs, :]
+    live = (floats((segs, 1), 0) < count_in[...].astype(jnp.float32)).astype(jnp.float32)
+    sums = live * jnp.sum(weights, axis=1, keepdims=True)
+    ids_col = up[0:segs, 3 * segs : 3 * segs + 1]
+    def_col = up[0:segs, 3 * segs + 1 : 3 * segs + 2]
+    at_lane = floats((segs, 128), 1)
+    hot = jnp.where(ids_col == at_lane, 1.0, 0.0)
+    tile[...] = jnp.where(
+        at_lane == DEFOCUS,
+        def_col,
+        jnp.where(at_lane == TOTAL, sums, jnp.where(at_lane == LIVE, live, hot)),
+    )
     tile_copies = [to_fil(k, tile, tiles_all, tile_send, tile_recv) for k in range(1, fils)]
-    ref_copies = [to_fil(k, refs, refs_all, ref_send, ref_recv) for k in range(1, fils)]
-    for c in tile_copies + ref_copies:
+    for c in tile_copies:
         c.start()
     tiles_all[fil] = tile[...]
-    refs_all[fil] = refs[...]
 
     pairs = segs * SHIFTS
-    sy = cols[:, 0:1]
-    sx = cols[:, 1:2]
-    wt = cols[:, 2:3]
+
+    def column(j):
+        first = j * segs
+        return jnp.concatenate(
+            [up[0:SHIFTS, first + i : first + i + 1] for i in range(segs)], axis=0
+        )
+
+    sy, sx, wt = column(0), column(1), column(2)
     lane = lax.broadcasted_iota(jnp.int32, (1, 2 * rows), 1)
     ky = (row * rows + lax.rem(lane, rows)).astype(jnp.float32)
     kw = jnp.where(ky >= box // 2, ky - box, ky)
@@ -260,6 +330,7 @@
     kyl = (row * rows).astype(jnp.float32) + floats((rows, 1), 0)
     kwl = jnp.where(kyl >= box // 2, kyl - box, kyl)
     gains = []
+    pulls[5].wait()
     for i in range(segs):
         ctf = ctf_of(tile[i : i + 1, DEFOCUS : DEFOCUS + 1], kwl, kx, box)
         g = ctf * tile[i : i + 1, LIVE : LIVE + 1]
@@ -282,7 +353,7 @@
             pf[d, pl.ds(segs + i, own, stride=2 * segs), :] = p_im[part]
 
     p_copies = []
-    for k in range(1, fils):
+    for k in sorted(range(1, fils), key=lambda k: abs(k - fils // 2)):
         d = fil_peer(k)
         pbuf[d] = pf[d].astype(jnp.bfloat16)
         c = to_fil(k, pbuf.at[d], precv, p_send, p_recv)
@@ -290,8 +361,48 @@
         p_copies.append(c)
     precv[fil] = pf[fil].astype(jnp.bfloat16)
 
+    for k in range(2, fils, 2):
+        from_fil(k, refs_all, ref_send, ref_recv).wait_recv()
+        d = fil_peer(k)
+        c = pltpu.make_async_remote_copy(
+            src_ref=refs_all.at[d],
+            dst_ref=refs_all.at[d],
+            send_sem=ref_send.at[fils // 2 + k // 2],
+            recv_sem=ref_recv.at[d],
+            device_id=(partner, row),
+            device_id_type=MESH,
+        )
+        c.start()
+        ref_copies.append(c)
+
     for k in range(1, fils):
-        from_fil(k, refs_all, ref_send, ref_recv).wait_recv()
+        from_fil(k, tiles_all, tile_send, tile_recv).wait_recv()
+    every = fils * segs
+    tiles = tiles_all[...].reshape(every, 128)
+    member = jnp.transpose(tiles)[:CLASSES].astype(jnp.bfloat16)
+    defocus = tiles[:, DEFOCUS : DEFOCUS + 1]
+    total = tiles[:, TOTAL : TOTAL + 1]
+    squares = []
+    for y in range(own):
+        k0 = (row * rows + fil * own + y).astype(jnp.float32)
+        k0 = jnp.where(k0 >= box // 2, k0 - box, k0)
+        ctf = ctf_of(defocus, k0, kx, box)
+        squares.append(total * (ctf * ctf))
+    d_hi, d_lo = split(jnp.concatenate(squares, axis=1))
+    denom = mm(member, d_hi) + mm(member, d_lo)
+    scale = lax.rsqrt(denom + 1.0)
+
+    pulls[6].wait()
+    for k in range(0, fils // 2):
+        d = lax.rem(partner + 2 * k, fils)
+        pltpu.make_async_remote_copy(
+            src_ref=refs_all.at[d],
+            dst_ref=refs_all.at[d],
+            send_sem=ref_send.at[0],
+            recv_sem=ref_recv.at[d],
+            device_id=(partner, row),
+            device_id_type=MESH,
+        ).wait_recv()
     for i in range(segs):
         at = slice(i * SHIFTS, (i + 1) * SHIFTS)
         lhs = jnp.concatenate([a_hi[at], b_hi[at], a_lo[at], b_lo[at]], axis=0)
@@ -340,23 +451,6 @@
         s_copies.append(c)
 
     for k in range(1, fils):
-        from_fil(k, tiles_all, tile_send, tile_recv).wait_recv()
-    every = fils * segs
-    tiles = tiles_all[...].reshape(every, 128)
-    member = jnp.transpose(tiles)[:CLASSES].astype(jnp.bfloat16)
-    defocus = tiles[:, DEFOCUS : DEFOCUS + 1]
-    total = tiles[:, TOTAL : TOTAL + 1]
-    squares = []
-    for y in range(own):
-        k0 = (row * rows + fil * own + y).astype(jnp.float32)
-        k0 = jnp.where(k0 >= box // 2, k0 - box, k0)
-        ctf = ctf_of(defocus, k0, kx, box)
-        squares.append(total * (ctf * ctf))
-    d_hi, d_lo = split(jnp.concatenate(squares, axis=1))
-    denom = mm(member, d_hi) + mm(member, d_lo)
-    scale = lax.rsqrt(denom + 1.0)
-
-    for k in range(1, fils):
         from_fil(k, precv, p_send, p_recv).wait_recv()
     parts = precv[...].astype(jnp.float32).reshape(fils, 2 * own, segs, kcols)
     for y in range(own):
@@ -388,17 +482,11 @@
     segs, _, rows, kcols = images.shape
     fils = lax.axis_size("fil")
     row_devs = lax.axis_size("row")
-    live = (jnp.arange(SEG_FIL, dtype=jnp.int32) < seg_count).astype(jnp.float32)
-    weight = posterior.astype(jnp.float32) / 256.0
-    member = (class_ids[:, None] == jnp.arange(CLASSES, dtype=jnp.int32)[None]).astype(jnp.float32)
-    numbers = jnp.stack([defocus, live * jnp.sum(weight, axis=1), live], axis=1)
-    tile = jnp.pad(jnp.concatenate([member, numbers], axis=1), ((0, 0), (0, 125 - CLASSES)))
-    shifts = offsets.astype(jnp.float32).reshape(segs * SHIFTS, 2)
-    cols = jnp.concatenate([shifts, weight.reshape(segs * SHIFTS, 1)], axis=1)
     own = rows // fils
     block = 2 * own * segs
     per = SHIFTS // row_devs
     vmem = pl.BlockSpec(memory_space=pltpu.VMEM)
+    hbm = pl.BlockSpec(memory_space=pl.ANY)
     dma = pltpu.SemaphoreType.DMA
 
     def kernel(*refs):
@@ -410,9 +498,17 @@
             jax.ShapeDtypeStruct((segs, 128), jnp.float32),
             jax.ShapeDtypeStruct((CLASSES, 2 * own * kcols), jnp.float32),
         ),
-        in_specs=[vmem] * 4,
+        in_specs=[hbm] * 7,
         out_specs=(vmem, vmem),
         scratch_shapes=[
+            pltpu.VMEM(images.shape, images.dtype),
+            pltpu.VMEM((segs, 2, SHIFTS), jnp.int32),
+            pltpu.VMEM((segs, SHIFTS), jnp.int32),
+            pltpu.VMEM((1, segs), jnp.float32),
+            pltpu.VMEM((1, segs), jnp.int32),
+            pltpu.VMEM((1, 1), jnp.int32),
+            pltpu.VMEM((128, 128), jnp.float32),
+            pltpu.VMEM((segs, 128), jnp.float32),
             pltpu.VMEM((fils, 2, rows, kcols), jnp.bfloat16),
             pltpu.VMEM((fils, segs, 128), jnp.float32),
             pltpu.VMEM((fils, block, kcols), jnp.float32),
@@ -430,11 +526,20 @@
             dma((fils,)),
             dma((row_devs,)),
             dma((row_devs,)),
+            dma((7,)),
         ],
         compiler_params=pltpu.CompilerParams(
-            collective_id=0, has_side_effects=True, vmem_limit_bytes=32 * 1024 * 1024
+            collective_id=0, has_side_effects=True, vmem_limit_bytes=60 * 1024 * 1024
         ),
-    )(images, references[0], tile, cols)
+    )(
+        images,
+        references[0],
+        jnp.transpose(offsets, (0, 2, 1)),
+        posterior,
+        defocus[None],
+        class_ids[None],
+        seg_count[None],
+    )
     return scores[:, : per * fils].reshape(segs, per, fils), averages
 
 

time: 27 us -> 26.6 us (0.985)
  the two profiles are of different devices: /device:TPU:27 before, /device:TPU:0 now
where the time goes in v2:
time: 26.6 us; the launch traced here: 26.4 us
  Pallas kernels  22.2 us (83%)
  local copies, waits for them, and re-layouts  2.92 us (11%)
  between operations  1.3 us (5%)
    pallas_call x1, Pallas kernels, per_device_fused(): pl.pallas_call(kernel, out_shape=(jax.ShapeDtypeStruct((segs, 128), jnp.f...  22.2 us
    unnamed x3, local copies, waits for them, and re-layouts  2.23 us
    reshape x1, local copies, waits for them, and re-layouts, per_device_fused(): return (scores[:, :per * fils].reshape(segs, per, fils), averages)  0.69 us

profile of v2, /device:TPU:0, one launch (start us, length us, event | category | flops | bytes accessed | tf_op | source)
XLA Modules:
  0.0 26.4 jit_solution(5388971274439232301)
XLA Ops:
  1.3 22.2 %shard_map.86 = (f32[8,128]{1,0:T(8,128)}, f32[16,2048]{1,0:T(8,128)}) custom-call(bf16[8,2,64,128]{3,2,1,0:T(8,128)(2,1)} %refs_0_.1, bf16[2,64,128]{2,1,0:T(8,128)(2,1)} %bitcast.7, s32[8,2,32]{2,1,0:T(2,128)} %bitcast.8, s32[8,32]{1,0:T(8,128)} %refs_3_.1, f32[1,8]{1,0:T(1,128)} %bitcast.10, s32[1,8]{1,0:T(1,128)} %bitcast.11, s32[1,1]{1,0:T(1,128)} %bitcast.6.refs_6_), custom_call_target="tpu_custom_call" | custom-call | tf_op jit(solution)/shard_map/pallas_call | solution.py:495
  23.5 0.0 copy-start
  23.5 0.7 %copy-done = f32[8,128]{1,0:T(8,128)S(1)} copy-done((f32[8,128]{1,0:T(8,128)S(1)}, f32[8,128]{1,0:T(8,128)}, u32[]{:S(2)}) %copy-start) | copy-done | bytes 4120
  24.2 0.7 %reshape.7 = f32[8,8,8]{2,1,0:T(8,128)} reshape(f32[8,64]{1,0:T(8,128)S(1)} %bitcast.9) | data formatting | bytes 4096 | tf_op jit(solution)/shard_map/reshape | solution.py:543
  24.9 1.6 %copy.11 = f32[16,2048]{1,0:T(8,128)} copy(f32[16,2048]{1,0:T(8,128)} %get-tuple-element.9) | data formatting | bytes 262144
Async XLA Ops:
  23.5 0.7 %copy-start = (f32[8,128]{1,0:T(8,128)S(1)}, f32[8,128]{1,0:T(8,128)}, u32[]{:S(2)}) copy-start(f32[8,128]{1,0:T(8,128)} %get-tuple-element.4) | copy-start | bytes 12292

commit v3 on v2

--- a/solution.py
+++ b/solution.py
@@ -130,11 +130,12 @@
     41.37130756865165,
     -12.514333309608835,
 )
+NEAREST = 12582912.0
 DEFOCUS, TOTAL, LIVE = 16, 17, 18
 
 
 def sine_turns(turns):
-    r = turns - jnp.round(turns)
+    r = turns - ((turns + NEAREST) - NEAREST)
     z = r * r
     p = jnp.full_like(z, SINE[-1])
     for c in SINE[-2::-1]:
@@ -235,7 +236,6 @@
     ]
     for c in pulls:
         c.start()
-    pl.semaphore_wait(barrier, fils + row_devs - 2)
 
     def to_fil(k, src, dst_all, send, recv):
         return pltpu.make_async_remote_copy(
@@ -257,23 +257,6 @@
             device_id=(d, row),
             device_id_type=MESH,
         )
-
-    partner = fil + 1 - 2 * lax.rem(fil, 2)
-    ref_copies = []
-    for k in range(fils // 2, 0, -1):
-        d = fil_peer(2 * k) if 2 * k < fils else partner
-        ref_copies.append(
-            pltpu.make_async_remote_copy(
-                src_ref=refs,
-                dst_ref=refs_all.at[fil],
-                send_sem=ref_send.at[k],
-                recv_sem=ref_recv.at[fil],
-                device_id=(d, row),
-                device_id_type=MESH,
-            )
-        )
-    for c in ref_copies:
-        c.start()
 
     for c in pulls[:5]:
         c.wait()
@@ -297,9 +280,6 @@
         def_col,
         jnp.where(at_lane == TOTAL, sums, jnp.where(at_lane == LIVE, live, hot)),
     )
-    tile_copies = [to_fil(k, tile, tiles_all, tile_send, tile_recv) for k in range(1, fils)]
-    for c in tile_copies:
-        c.start()
     tiles_all[fil] = tile[...]
 
     pairs = segs * SHIFTS
@@ -322,6 +302,27 @@
     qc = -(sx * kx)
     col_cos = sine_turns((qc + 64.0) * (1.0 / box))
     col_sin = sine_turns(qc * (1.0 / box))
+
+    pl.semaphore_wait(barrier, fils + row_devs - 2)
+    partner = fil + 1 - 2 * lax.rem(fil, 2)
+    ref_copies = []
+    for k in range(fils // 2, 0, -1):
+        d = fil_peer(2 * k) if 2 * k < fils else partner
+        ref_copies.append(
+            pltpu.make_async_remote_copy(
+                src_ref=refs,
+                dst_ref=refs_all.at[fil],
+                send_sem=ref_send.at[k],
+                recv_sem=ref_recv.at[fil],
+                device_id=(d, row),
+                device_id_type=MESH,
+            )
+        )
+    for c in ref_copies:
+        c.start()
+    tile_copies = [to_fil(k, tile, tiles_all, tile_send, tile_recv) for k in range(1, fils)]
+    for c in tile_copies:
+        c.start()
 
     a_hi, a_lo = split(wave_a)
     b_hi, b_lo = split(wave_b)
@@ -423,10 +424,13 @@
                     col_cos[at] * ze[:SHIFTS] - col_sin[at] * ze[SHIFTS:]
                 )
     f_hi, f_lo = split(fbuf[...])
-    wide = (fils * kcols, 128)
-    ones = (
-        lax.broadcasted_iota(jnp.int32, wide, 0) // kcols
-        == lax.rem(lax.broadcasted_iota(jnp.int32, wide, 1), fils)
+    lane = lax.broadcasted_iota(jnp.int32, (1, 128), 1)
+    ones = jnp.concatenate(
+        [
+            jnp.broadcast_to((lane & (fils - 1) == r).astype(jnp.float32), (kcols, 128))
+            for r in range(fils)
+        ],
+        axis=0,
     ).astype(jnp.bfloat16)
     spread = mm(f_hi, ones) + mm(f_lo, ones)
     per = SHIFTS // row_devs
@@ -486,7 +490,7 @@
     block = 2 * own * segs
     per = SHIFTS // row_devs
     vmem = pl.BlockSpec(memory_space=pltpu.VMEM)
-    hbm = pl.BlockSpec(memory_space=pl.ANY)
+    hbm = pl.BlockSpec(memory_space=pltpu.HBM)
     dma = pltpu.SemaphoreType.DMA
 
     def kernel(*refs):
@@ -529,7 +533,7 @@
             dma((7,)),
         ],
         compiler_params=pltpu.CompilerParams(
-            collective_id=0, has_side_effects=True, vmem_limit_bytes=60 * 1024 * 1024
+            collective_id=0, has_side_effects=True, vmem_limit_bytes=32 * 1024 * 1024
         ),
     )(
         images,

time: 26.6 us -> 27.2 us (1.023)
  local copies, waits for them, and re-layouts: 2.92 us -> 4.4 us
  Pallas kernels: 22.2 us -> 21.2 us
    unnamed x3 -> x13, local copies, waits for them, and re-layouts: 2.23 us -> 3.71 us
    pallas_call x1, Pallas kernels: 22.2 us -> 21.2 us  [per_device_fused(): pl.pallas_call(kernel, out_shape=(jax.ShapeDtypeStruct((segs, 128), jnp.f...]
where the time goes in v3:
time: 27.2 us; the launch traced here: 26.9 us
  Pallas kernels  21.2 us (78%)
  local copies, waits for them, and re-layouts  4.4 us (16%)
  between operations  1.33 us (5%)
    pallas_call x1, Pallas kernels, per_device_fused(): pl.pallas_call(kernel, out_shape=(jax.ShapeDtypeStruct((segs, 128), jnp.f...  21.2 us
    unnamed x13, local copies, waits for them, and re-layouts  3.71 us
    reshape x1, local copies, waits for them, and re-layouts, per_device_fused(): return (scores[:, :per * fils].reshape(segs, per, fils), averages)  0.69 us

profile of v3, /device:TPU:0, one launch (start us, length us, event | category | flops | bytes accessed | tf_op | source)
XLA Modules:
  0.0 26.9 jit_solution(255692419393244799)
XLA Ops:
  0.6 0.0 copy-start.2
  1.3 0.0 copy-start.4
  1.3 0.0 copy-start.5
  1.3 0.0 copy-done.2
  1.3 0.6 %copy-done.4 = f32[8]{0:T(128)S(1)} copy-done((f32[8]{0:T(128)S(1)}, f32[8]{0:T(128)}, u32[]{:S(2)}) %copy-start.4) | copy-done | bytes 56
  2.0 0.0 copy-done.5
  2.0 0.0 copy-start
  2.0 0.9 %copy-done = bf16[8,2,64,128]{3,2,1,0:T(8,128)(2,1)S(1)} copy-done((bf16[8,2,64,128]{3,2,1,0:T(8,128)(2,1)S(1)}, bf16[8,2,64,128]{3,2,1,0:T(8,128)(2,1)}, u32[]{:S(2)}) %copy-start) | copy-done | bytes 262168
  2.9 0.0 copy-start.1
  2.9 0.8 %copy-done.1 = bf16[1,2,64,128]{3,2,1,0:T(8,128)(2,1)S(1)} copy-done((bf16[1,2,64,128]{3,2,1,0:T(8,128)(2,1)S(1)}, bf16[1,2,64,128]{3,2,1,0:T(8,128)(2,1)}, u32[]{:S(2)}) %copy-start.1) | copy-done | bytes 32792
  3.7 0.0 copy-start.3
  3.7 0.7 %copy-done.3 = s32[8,32]{1,0:T(8,128)S(1)} copy-done((s32[8,32]{1,0:T(8,128)S(1)}, s32[8,32]{1,0:T(8,128)}, u32[]{:S(2)}) %copy-start.3) | copy-done | bytes 1048
  4.4 21.2 %shard_map.86 = (f32[8,128]{1,0:T(8,128)S(1)}, f32[16,2048]{1,0:T(8,128)S(1)}) custom-call(bf16[8,2,64,128]{3,2,1,0:T(8,128)(2,1)S(1)} %copy-done, bf16[2,64,128]{2,1,0:T(8,128)(2,1)S(1)} %bitcast.7, s32[8,2,32]{2,1,0:T(2,128)S(1)} %bitcast.8, s32[8,32]{1,0:T(8,128)S(1)} %copy-done.3, f32[1,8]{1,0:T(1,128)S(1)} %bitcast.10, s32[1,8]{1,0:T(1,128)S(1)} %bitcast.11, ...), custom_call_target="tpu_custom_call" | custom-call | tf_op jit(solution)/shard_map/pallas_call | solution.py:499
  25.6 0.7 %reshape.7 = f32[8,8,8]{2,1,0:T(8,128)} reshape(f32[8,64]{1,0:T(8,128)S(1)} %bitcast.9) | data formatting | bytes 4096 | tf_op jit(solution)/shard_map/reshape | solution.py:547
  26.3 0.7 %copy.11 = f32[16,2048]{1,0:T(8,128)} copy(f32[16,2048]{1,0:T(8,128)S(1)} %get-tuple-element.9) | data formatting | bytes 262144
Async XLA Ops:
  0.6 0.7 %copy-start.2 = (s32[8,32,2]{1,2,0:T(2,128)S(1)}, s32[8,32,2]{1,2,0:T(2,128)}, u32[]{:S(2)}) copy-start(s32[8,32,2]{1,2,0:T(2,128)} %param.10) | copy-start | bytes 6148
  1.3 0.7 %copy-start.4 = (f32[8]{0:T(128)S(1)}, f32[8]{0:T(128)}, u32[]{:S(2)}) copy-start(f32[8]{0:T(128)} %param.8) | copy-start | bytes 100
  1.3 0.7 %copy-start.5 = (s32[8]{0:T(128)S(1)}, s32[8]{0:T(128)}, u32[]{:S(2)}) copy-start(s32[8]{0:T(128)} %param.12) | copy-start | bytes 100
  2.0 0.9 %copy-start = (bf16[8,2,64,128]{3,2,1,0:T(8,128)(2,1)S(1)}, bf16[8,2,64,128]{3,2,1,0:T(8,128)(2,1)}, u32[]{:S(2)}) copy-start(bf16[8,2,64,128]{3,2,1,0:T(8,128)(2,1)} %refs_0_.1) | copy-start | bytes 786436
  2.9 0.8 %copy-start.1 = (bf16[1,2,64,128]{3,2,1,0:T(8,128)(2,1)S(1)}, bf16[1,2,64,128]{3,2,1,0:T(8,128)(2,1)}, u32[]{:S(2)}) copy-start(bf16[1,2,64,128]{3,2,1,0:T(8,128)(2,1)} %param.9) | copy-start | bytes 98308
  3.7 0.7 %copy-start.3 = (s32[8,32]{1,0:T(8,128)S(1)}, s32[8,32]{1,0:T(8,128)}, u32[]{:S(2)}) copy-start(s32[8,32]{1,0:T(8,128)} %refs_3_.1) | copy-start | bytes 3076

commit v4 on v3

--- a/solution.py
+++ b/solution.py
@@ -297,7 +297,6 @@
     low = lane < rows
     q = -(sy * kw)
     wave_a = sine_turns((q + jnp.where(low, 64.0, 128.0)) * (1.0 / box))
-    wave_b = sine_turns((q + jnp.where(low, 0.0, 64.0)) * (1.0 / box))
     kx = floats((1, kcols), 1)
     qc = -(sx * kx)
     col_cos = sine_turns((qc + 64.0) * (1.0 / box))
@@ -325,7 +324,6 @@
         c.start()
 
     a_hi, a_lo = split(wave_a)
-    b_hi, b_lo = split(wave_b)
     c_hi, c_lo = split(jnp.concatenate([col_cos * wt, col_sin * wt], axis=1))
 
     kyl = (row * rows).astype(jnp.float32) + floats((rows, 1), 0)
@@ -393,6 +391,8 @@
     denom = mm(member, d_hi) + mm(member, d_lo)
     scale = lax.rsqrt(denom + 1.0)
 
+    wave_b = sine_turns((q + jnp.where(low, 0.0, 64.0)) * (1.0 / box))
+    b_hi, b_lo = split(wave_b)
     pulls[6].wait()
     for k in range(0, fils // 2):
         d = lax.rem(partner + 2 * k, fils)
@@ -477,9 +477,19 @@
             device_id_type=MESH,
         ).wait_recv()
         acc = acc + srecv[q]
-    scores_out[...] = acc
+    for j in range(per):
+        scores_out[:, j, :] = acc[:, j * fils : (j + 1) * fils]
     for c in tile_copies + ref_copies + p_copies + s_copies:
         c.wait_send()
+
+
+def hand_over(scores, averages, scores_out, avg_out, sem):
+    first = pltpu.make_async_copy(averages, avg_out, sem.at[0])
+    second = pltpu.make_async_copy(scores, scores_out, sem.at[1])
+    first.start()
+    second.start()
+    first.wait()
+    second.wait()
 
 
 def per_device_fused(images, defocus, references, offsets, posterior, class_ids, seg_count):
@@ -490,7 +500,7 @@
     block = 2 * own * segs
     per = SHIFTS // row_devs
     vmem = pl.BlockSpec(memory_space=pltpu.VMEM)
-    hbm = pl.BlockSpec(memory_space=pltpu.HBM)
+    hbm = pl.BlockSpec(memory_space=pl.ANY)
     dma = pltpu.SemaphoreType.DMA
 
     def kernel(*refs):
@@ -499,7 +509,7 @@
     scores, averages = pl.pallas_call(
         kernel,
         out_shape=(
-            jax.ShapeDtypeStruct((segs, 128), jnp.float32),
+            jax.ShapeDtypeStruct((segs, per, fils), jnp.float32),
             jax.ShapeDtypeStruct((CLASSES, 2 * own * kcols), jnp.float32),
         ),
         in_specs=[hbm] * 7,
@@ -533,7 +543,7 @@
             dma((7,)),
         ],
         compiler_params=pltpu.CompilerParams(
-            collective_id=0, has_side_effects=True, vmem_limit_bytes=32 * 1024 * 1024
+            collective_id=0, has_side_effects=True, vmem_limit_bytes=60 * 1024 * 1024
         ),
     )(
         images,
@@ -544,7 +554,17 @@
         class_ids[None],
         seg_count[None],
     )
-    return scores[:, : per * fils].reshape(segs, per, fils), averages
+    return pl.pallas_call(
+        hand_over,
+        out_shape=(
+            jax.ShapeDtypeStruct(scores.shape, scores.dtype),
+            jax.ShapeDtypeStruct(averages.shape, averages.dtype),
+        ),
+        in_specs=[hbm] * 2,
+        out_specs=(hbm, hbm),
+        scratch_shapes=[dma((2,))],
+        compiler_params=pltpu.CompilerParams(vmem_limit_bytes=60 * 1024 * 1024),
+    )(scores, averages)
 
 
 def fits(mesh):

time: 27.2 us -> 29.9 us (1.099)
  Pallas kernels: 21.2 us -> 28.4 us
  local copies, waits for them, and re-layouts: 4.4 us -> 0 us
    pallas_call x1 -> x2, Pallas kernels: 21.2 us -> 28.4 us  [the longest x1 22.3 us: per_device_fused(): pl.pallas_call(kernel, out_shape=(jax.ShapeDtypeStruct((segs, per, fils),...]
    unnamed x13 -> x0, local copies, waits for them, and re-layouts: 3.71 us -> none
    reshape x1 -> x0, local copies, waits for them, and re-layouts: 0.69 us -> none  [per_device_fused(): return (scores[:, :per * fils].reshape(segs, per, fils), averages)]
where the time goes in v4:
time: 29.9 us; the launch traced here: 29.7 us
  Pallas kernels  28.4 us (95%)
  between operations  1.29 us (4%)
    pallas_call x1, Pallas kernels, per_device_fused(): pl.pallas_call(kernel, out_shape=(jax.ShapeDtypeStruct((segs, per, fils),...  22.3 us
    pallas_call x1, Pallas kernels, per_device_fused(): pl.pallas_call(hand_over, out_shape=(jax.ShapeDtypeStruct(scores.shape, s...  6.08 us

profile of v4, /device:TPU:0, one launch (start us, length us, event | category | flops | bytes accessed | tf_op | source)
XLA Modules:
  0.0 29.7 jit_solution(13920339072481399557)
XLA Ops:
  1.3 22.3 %shard_map.86 = (f32[8,8,8]{2,1,0:T(8,128)}, f32[16,2048]{1,0:T(8,128)}) custom-call(bf16[8,2,64,128]{3,2,1,0:T(8,128)(2,1)} %refs_0_.1, bf16[2,64,128]{2,1,0:T(8,128)(2,1)} %bitcast.6, s32[8,2,32]{2,1,0:T(2,128)} %bitcast.7, s32[8,32]{1,0:T(8,128)} %refs_3_.1, f32[1,8]{1,0:T(1,128)} %bitcast.8, s32[1,8]{1,0:T(1,128)} %bitcast.9, s32[1,1]{1,0:T(1,128)} %bitcast.5.refs_6_), custom_call_target="tpu_custom_call" | custom-call | tf_op jit(solution)/shard_map/pallas_call | solution.py:509
  23.6 6.1 %shard_map.87 = (f32[8,8,8]{2,1,0:T(8,128)}, f32[16,2048]{1,0:T(8,128)}) custom-call(f32[8,8,8]{2,1,0:T(8,128)} %get-tuple-element.4.scores, f32[16,2048]{1,0:T(8,128)} %get-tuple-element.5.averages), custom_call_target="tpu_custom_call" | custom-call | tf_op jit(solution)/shard_map/pallas_call | solution.py:557

commit v5 on v4

--- a/solution.py
+++ b/solution.py
@@ -483,13 +483,9 @@
         c.wait_send()
 
 
-def hand_over(scores, averages, scores_out, avg_out, sem):
-    first = pltpu.make_async_copy(averages, avg_out, sem.at[0])
-    second = pltpu.make_async_copy(scores, scores_out, sem.at[1])
-    first.start()
-    second.start()
-    first.wait()
-    second.wait()
+def hand_over(scores, averages, scores_out, avg_out):
+    scores_out[...] = scores[...]
+    avg_out[...] = averages[...]
 
 
 def per_device_fused(images, defocus, references, offsets, posterior, class_ids, seg_count):
@@ -560,9 +556,8 @@
             jax.ShapeDtypeStruct(scores.shape, scores.dtype),
             jax.ShapeDtypeStruct(averages.shape, averages.dtype),
         ),
-        in_specs=[hbm] * 2,
-        out_specs=(hbm, hbm),
-        scratch_shapes=[dma((2,))],
+        in_specs=[vmem] * 2,
+        out_specs=(vmem, vmem),
         compiler_params=pltpu.CompilerParams(vmem_limit_bytes=60 * 1024 * 1024),
     )(scores, averages)
 

time: 29.9 us -> 25.4 us (0.85)
  Pallas kernels: 28.4 us -> 23.9 us
    pallas_call x1, Pallas kernels: 6.08 us -> 1.59 us  [per_device_fused(): pl.pallas_call(hand_over, out_shape=(jax.ShapeDtypeStruct(scores.shape, s...]
where the time goes in v5:
time: 25.4 us; the launch traced here: 25.2 us
  Pallas kernels  23.9 us (94%)
  between operations  1.29 us (5%)
    pallas_call x1, Pallas kernels, per_device_fused(): pl.pallas_call(kernel, out_shape=(jax.ShapeDtypeStruct((segs, per, fils),...  22.3 us
    pallas_call x1, Pallas kernels, per_device_fused(): pl.pallas_call(hand_over, out_shape=(jax.ShapeDtypeStruct(scores.shape, s...  1.59 us

profile of v5, /device:TPU:0, one launch (start us, length us, event | category | flops | bytes accessed | tf_op | source)
XLA Modules:
  0.0 25.2 jit_solution(5435047146312922304)
XLA Ops:
  1.3 22.3 %shard_map.86 = (f32[8,8,8]{2,1,0:T(8,128)}, f32[16,2048]{1,0:T(8,128)}) custom-call(bf16[8,2,64,128]{3,2,1,0:T(8,128)(2,1)} %refs_0_.1, bf16[2,64,128]{2,1,0:T(8,128)(2,1)} %bitcast.6, s32[8,2,32]{2,1,0:T(2,128)} %bitcast.7, s32[8,32]{1,0:T(8,128)} %refs_3_.1, f32[1,8]{1,0:T(1,128)} %bitcast.8, s32[1,8]{1,0:T(1,128)} %bitcast.9, s32[1,1]{1,0:T(1,128)} %bitcast.5.refs_6_), custom_call_target="tpu_custom_call" | custom-call | tf_op jit(solution)/shard_map/pallas_call | solution.py:505
  23.6 1.6 %shard_map.87 = (f32[8,8,8]{2,1,0:T(8,128)}, f32[16,2048]{1,0:T(8,128)}) custom-call(f32[8,8,8]{2,1,0:T(8,128)} %get-tuple-element.4.scores, f32[16,2048]{1,0:T(8,128)} %get-tuple-element.5.averages), custom_call_target="tpu_custom_call" | custom-call | tf_op jit(solution)/shard_map/pallas_call | solution.py:553
